TPU v7x, 512 devices: a whole 4x4x16 slice. The times are simulated.
512 devices in a mesh: pipe: 8 (over x, core), dp: 64 (over y, z).
Axes of the slice: x: 4, y: 4, z: 16, core: 2. Of those that a mesh axis runs over, the one named last changes fastest.
Arguments:
- acts: bfloat16 [8, 8192, 8192], P('pipe', 'dp'), may hold values from -6 to 6
- incoming: bfloat16 [8, 8192, 8192], P('pipe', 'dp'), may hold values from -6 to 6
- proj_in: bfloat16 [64, 8192], P(None, 'dp'), may hold values from -0.0625 to 0.0625
- proj_out: bfloat16 [64, 8192], P(None, 'dp'), may hold values from -0.0625 to 0.0625
- valid_rows: bfloat16 [8, 128, 4096], P('pipe', 'dp'), may hold values from -0.09375 to 0.09375
- lengths: int32 [64], P('dp'), may hold values from 1 to 128, 7168 in all
- domains: int32 [64], replicated, may hold values from 0 to 63
Outputs:
- domain_gram: float32 [8, 64, 128, 128], P('pipe', 'dp')
All inputs are finite; a program needn't handle non-finite values. No bound on the sum of `lengths` on one device may be relied on, other than what follows from the above.
Results may differ from a plain program's by a relative error of at most 0.004.
Values may be sent and summed in bfloat16 or wider, within the bound.
No kernel may reach another device: no remote copies, remote signals or barrier semaphores. Data moves between devices by JAX's collectives and lax.ppermute only.
A program may use at most 128 MiB of HBM per device.

v0:
```python
import jax
import jax.numpy as jnp
from jax import lax
from jax.sharding import PartitionSpec as P

highest_precision = lax.Precision.HIGHEST


def entering(value, axis, combine, identity):
    length, place = (lax.axis_size(axis), lax.axis_index(axis))
    everything = lax.all_gather(value.astype(jnp.bfloat16), axis)
    start = jnp.broadcast_to(jnp.asarray(identity, value.dtype), value.shape)

    def lap(k, before):
        at = length - 1 - k
        reached = at > place
        new = combine(before, everything[at].astype(value.dtype))
        return jnp.where(reached, new, before)

    return lax.fori_loop(0, length, lap, start)


def add_terms(earlier, later):
    return earlier + later


def body(acts, incoming, proj_in, proj_out, valid_rows, lengths, domains):
    layer_act = acts[0]
    branch = incoming[0]
    rows_here = layer_act.shape[0]
    proj_size = proj_in.shape[0]
    grad_term = branch.astype(jnp.float32)
    above = entering(grad_term, "pipe", add_terms, jnp.zeros_like(grad_term))
    source = above + grad_term
    empty = jnp.zeros((rows_here, proj_size), jnp.float32)
    pieces = (
        lax.all_gather(proj_in, "dp", axis=1, tiled=True),
        lax.all_gather(proj_out, "dp", axis=1, tiled=True),
    )
    new_act = lax.dot_general(
        layer_act, pieces[0], (((1,), (1,)), ((), ())), preferred_element_type=jnp.float32
    )
    if source.dtype == jnp.float32:
        new_grad = (empty, empty)[1] + lax.dot_general(
            source,
            pieces[1].astype(jnp.float32),
            (((1,), (1,)), ((), ())),
            precision=highest_precision,
        )
    else:
        new_grad = lax.dot_general(
            source, pieces[1], (((1,), (1,)), ((), ())), preferred_element_type=jnp.float32
        )
    live_count = lengths[0]
    positions = lax.iota(jnp.int32, rows_here)
    weights = jnp.where(positions < live_count, 1.0, 0.0).astype(jnp.float32) / live_count.astype(
        jnp.float32
    )
    scaled = new_grad * weights[:, None]
    grad_row = lax.dot_general(
        scaled, new_act, (((0,), (0,)), ((), ())), precision=highest_precision
    )
    grad_row = grad_row.reshape(1, proj_size * proj_size).astype(jnp.bfloat16)
    valid_full = lax.all_gather(valid_rows, "dp", axis=1, tiled=True)[0]
    my_index = lax.axis_index("dp")
    scores = lax.dot_general(
        lax.all_gather(grad_row, "dp", axis=0, tiled=True),
        valid_full,
        (((1,), (1,)), ((), ())),
        preferred_element_type=jnp.float32,
    )
    owned = domains == my_index
    kept = scores * owned.astype(jnp.float32)[:, None]
    gram = lax.dot_general(kept, scores, (((0,), (0,)), ((), ())), precision=highest_precision)
    return gram[None, None]


def solution(mesh):
    placed = (
        P("pipe", "dp", None),
        P("pipe", "dp", None),
        P(None, "dp"),
        P(None, "dp"),
        P("pipe", "dp", None),
        P("dp"),
        P(),
    )
    return jax.shard_map(
        body, mesh=mesh, in_specs=placed, out_specs=P("pipe", "dp", None, None), check_vma=False
    )
```

profile of v0, /device:TPU:4, one launch (start us, length us, event | category | flops | bytes accessed | tf_op | source)
XLA Modules:
  0.0 522.5 jit_solution(17948236121018723122)
XLA Ops:
  6.5 0.0 copy-start
  6.5 0.0 all-gather.10.cloned.1.call-start
  6.5 0.7 all-gather.10.cloned.1.call-update
  7.3 0.0 all-gather.6.cloned.1.call-start
  7.3 0.7 all-gather.6.cloned.1.call-update
  8.0 0.0 all-gather.8.cloned.1.call-start
  8.1 0.7 all-gather.8.cloned.1.call-update
  8.7 0.0 all-gather.12.cloned.1.call-start
  8.8 1.4 copy.10
  10.1 0.0 all-gather.12.cloned.1.call-update
  10.9 0.7 compare_convert_fusion
  11.5 134.6 %all-gather.10.cloned.1.call-done = bf16[64,8192]{1,0:T(8,128)(2,1)} async-done(((bf16[64,128]{1,0:T(8,128)(2,1)}), bf16[64,8192]{1,0:T(8,128)(2,1)}) %all-gather.10.cloned.1.call-update) | async-done | bytes 1048592 | tf_op jit(solution)/shard_map/all_gather | solution.py:37
  146.1 0.0 copy-done
  146.1 2.1 fusion.2
  148.2 88.0 %all-gather.6.cloned.1.call-done = bf16[8,128,8192]{2,1,0:T(8,128)(2,1)} async-done(((bf16[1,128,8192]{2,1,0:T(8,128)(2,1)}), bf16[8,128,8192]{2,1,0:T(8,128)(2,1)}) %all-gather.6.cloned.1.call-update) | async-done | bytes 16777232 | tf_op jit(solution)/shard_map/all_gather | solution.py:11
  236.1 41.8 %while.16 = (s32[]{:T(128)}, f32[128,8192]{1,0:T(8,128)}, s32[]{:T(128)}, bf16[8,128,8192]{2,1,0:T(8,128)(2,1)}, s32[]{:T(128)}, /*index=5*/s32[]{:T(128)}, s32[]{:T(128)}, s32[]{:T(128)}) while((s32[]{:T(128)}, f32[128,8192]{1,0:T(8,128)}, s32[]{:T(128)}, bf16[8,128,8192]{2,1,0:T(8,128)(2,1)}, s32[]{:T(128)}, ...), condition=%wide.region_1.2_spmd.clone, body=%wide.region_0.1_spmd.clone.sunk | while | flops 4194312 | bytes 10485915 | solution.py:20
  236.1 4.1 add_select_fusion.2
  240.2 5.4 %add_select_fusion.2 = f32[128,8192]{1,0:T(8,128)} fusion(f32[128,8192]{1,0:T(8,128)} %get-tuple-element.173, bf16[8,128,8192]{2,1,0:T(8,128)(2,1)} %get-tuple-element.183, s32[]{:T(128)S(6)} %select_n.54, pred[]{:T(512)S(6)} %compare.3, pred[]{:T(512)S(6)} %gt.12), kind=kLoop, calls=%fused_computation.clone.1 | loop fusion | flops 4194304 | bytes 10485766 | tf_op jit(solution)/shard_map/while/body/eval_jaxpr/jit(_where)/select_n | solution.py:18
  245.6 5.4 %add_select_fusion.2 = f32[128,8192]{1,0:T(8,128)} fusion(f32[128,8192]{1,0:T(8,128)} %get-tuple-element.173, bf16[8,128,8192]{2,1,0:T(8,128)(2,1)} %get-tuple-element.183, s32[]{:T(128)S(6)} %select_n.54, pred[]{:T(512)S(6)} %compare.3, pred[]{:T(512)S(6)} %gt.12), kind=kLoop, calls=%fused_computation.clone.1 | loop fusion | flops 4194304 | bytes 10485766 | tf_op jit(solution)/shard_map/while/body/eval_jaxpr/jit(_where)/select_n | solution.py:18
  251.0 5.4 %add_select_fusion.2 = f32[128,8192]{1,0:T(8,128)} fusion(f32[128,8192]{1,0:T(8,128)} %get-tuple-element.173, bf16[8,128,8192]{2,1,0:T(8,128)(2,1)} %get-tuple-element.183, s32[]{:T(128)S(6)} %select_n.54, pred[]{:T(512)S(6)} %compare.3, pred[]{:T(512)S(6)} %gt.12), kind=kLoop, calls=%fused_computation.clone.1 | loop fusion | flops 4194304 | bytes 10485766 | tf_op jit(solution)/shard_map/while/body/eval_jaxpr/jit(_where)/select_n | solution.py:18
  256.4 5.4 %add_select_fusion.2 = f32[128,8192]{1,0:T(8,128)} fusion(f32[128,8192]{1,0:T(8,128)} %get-tuple-element.173, bf16[8,128,8192]{2,1,0:T(8,128)(2,1)} %get-tuple-element.183, s32[]{:T(128)S(6)} %select_n.54, pred[]{:T(512)S(6)} %compare.3, pred[]{:T(512)S(6)} %gt.12), kind=kLoop, calls=%fused_computation.clone.1 | loop fusion | flops 4194304 | bytes 10485766 | tf_op jit(solution)/shard_map/while/body/eval_jaxpr/jit(_where)/select_n | solution.py:18
  261.8 5.4 %add_select_fusion.2 = f32[128,8192]{1,0:T(8,128)} fusion(f32[128,8192]{1,0:T(8,128)} %get-tuple-element.173, bf16[8,128,8192]{2,1,0:T(8,128)(2,1)} %get-tuple-element.183, s32[]{:T(128)S(6)} %select_n.54, pred[]{:T(512)S(6)} %compare.3, pred[]{:T(512)S(6)} %gt.12), kind=kLoop, calls=%fused_computation.clone.1 | loop fusion | flops 4194304 | bytes 10485766 | tf_op jit(solution)/shard_map/while/body/eval_jaxpr/jit(_where)/select_n | solution.py:18
  267.1 5.4 %add_select_fusion.2 = f32[128,8192]{1,0:T(8,128)} fusion(f32[128,8192]{1,0:T(8,128)} %get-tuple-element.173, bf16[8,128,8192]{2,1,0:T(8,128)(2,1)} %get-tuple-element.183, s32[]{:T(128)S(6)} %select_n.54, pred[]{:T(512)S(6)} %compare.3, pred[]{:T(512)S(6)} %gt.12), kind=kLoop, calls=%fused_computation.clone.1 | loop fusion | flops 4194304 | bytes 10485766 | tf_op jit(solution)/shard_map/while/body/eval_jaxpr/jit(_where)/select_n | solution.py:18
  272.5 5.4 %add_select_fusion.2 = f32[128,8192]{1,0:T(8,128)} fusion(f32[128,8192]{1,0:T(8,128)} %get-tuple-element.173, bf16[8,128,8192]{2,1,0:T(8,128)(2,1)} %get-tuple-element.183, s32[]{:T(128)S(6)} %select_n.54, pred[]{:T(512)S(6)} %compare.3, pred[]{:T(512)S(6)} %gt.12), kind=kLoop, calls=%fused_computation.clone.1 | loop fusion | flops 4194304 | bytes 10485766 | tf_op jit(solution)/shard_map/while/body/eval_jaxpr/jit(_where)/select_n | solution.py:18
  277.9 93.9 %all-gather.8.cloned.1.call-done = bf16[64,8192]{1,0:T(8,128)(2,1)} async-done(((bf16[64,128]{1,0:T(8,128)(2,1)}), bf16[64,8192]{1,0:T(8,128)(2,1)}) %all-gather.8.cloned.1.call-update) | async-done | bytes 1048592 | tf_op jit(solution)/shard_map/all_gather | solution.py:38
  371.8 5.8 %fusion.4 = f32[128,64]{0,1:T(8,128)S(1)} fusion(bf16[64,8192]{1,0:T(8,128)(2,1)} %all-gather.8.cloned.1.call-done, f32[128,8192]{1,0:T(8,128)} %get-tuple-element.115, bf16[1,128,8192]{2,1,0:T(8,128)(2,1)} %param.10, f32[128]{0:T(128)S(1)} %fusion.12), kind=kOutput, calls=%fused_computation.7 | convolution fusion | flops 807411712 | bytes 7373312 | tf_op jit(solution)/shard_map/dot_general | solution.py:44
  377.6 0.2 convolution_convert_fusion
  377.8 0.1 reshape.28
  377.9 100.0 %all-gather = bf16[64,1,4096]{2,1,0:T(2,128)(2,1)S(1)} all-gather(bf16[1,1,4096]{2,1,0:T(2,128)(2,1)S(1)} %reshape.28), channel_id=1, replica_groups=mesh['pipe'=8,'dp'=64] {'dp'}, dimensions={0}, use_global_device_ids=true | all-gather | bytes 532480 | tf_op jit(solution)/shard_map/all_gather | solution.py:67
  477.8 33.8 %all-gather.12.cloned.1.call-done = bf16[1,128,4096]{2,0,1:T(2,128)(2,1)} async-done(((bf16[1,2,4096]{2,0,1:T(2,128)(2,1)}), bf16[1,128,4096]{2,0,1:T(2,128)(2,1)}) %all-gather.12.cloned.1.call-update) | async-done | bytes 1048592 | tf_op jit(solution)/shard_map/all_gather | solution.py:64
  511.7 3.3 fusion.5
  515.0 1.0 convolution_bitcast_fusion
  (2 shorter events, 0.0 us)
Async XLA Ops:
  6.5 139.6 %copy-start = (bf16[1,128,8192]{2,1,0:T(8,128)(2,1)S(1)}, bf16[1,128,8192]{2,1,0:T(8,128)(2,1)}, u32[]{:S(2)}) copy-start(bf16[1,128,8192]{2,1,0:T(8,128)(2,1)} %param.9) | copy-start | bytes 6291460
  6.5 139.6 %all-gather.10.cloned.1.call-start = ((), (), s32[]{:S(2)}) async-start(), calls=%async_computation.2 | async-start | bytes 1064960 | tf_op jit(solution)/shard_map/all_gather | solution.py:37
  7.3 228.9 %all-gather.6.cloned.1.call-start = ((), (), s32[]{:S(2)}) async-start(), calls=%async_computation | async-start | bytes 18874368 | tf_op jit(solution)/shard_map/all_gather | solution.py:11
  8.0 363.8 %all-gather.8.cloned.1.call-start = ((), (), s32[]{:S(2)}) async-start(), calls=%async_computation.1 | async-start | bytes 1064960 | tf_op jit(solution)/shard_map/all_gather | solution.py:38
  8.7 502.9 %all-gather.12.cloned.1.call-start = ((), (), s32[]{:S(2)}) async-start(), calls=%async_computation.3 | async-start | bytes 2129920 | tf_op jit(solution)/shard_map/all_gather | solution.py:64
Sparse Core Ops, SparseCore 0:
  10.3 135.7 all-gather.9
  148.3 87.8 all-gather.5
  239.1 132.7 all-gather.7
  374.6 137.0 all-gather.11
where the time goes:
time: 523 us
  waiting for transfers between devices  352 us (67%)
  blocking collectives  100 us (19%)
  other arithmetic  42.4 us (8%)
  between operations  13.8 us (3%)
  matrix products  12.3 us (2%)
    all_gather x1, waiting for transfers between devices, body(): lax.all_gather(proj_in, 'dp', axis=1, tiled=True)  135 us
    all_gather x1, blocking collectives, body(): lax.all_gather(grad_row, 'dp', axis=0, tiled=True)  100 us
    all_gather x1, waiting for transfers between devices, body(): lax.all_gather(proj_out, 'dp', axis=1, tiled=True)  93.9 us
    all_gather x1, waiting for transfers between devices, entering(): everything = lax.all_gather(value.astype(jnp.bfloat16), axis)  88 us
    select_n x8, other arithmetic, lap(): return jnp.where(reached, new, before)  41.8 us
    all_gather x1, waiting for transfers between devices, body(): valid_full = lax.all_gather(valid_rows, 'dp', axis=1, tiled=True)[0]  33.8 us
  transfers between devices with their start and end apart: 4, of which 4 were waited for; matrix products, arithmetic and copies ran while one was open for 10% of the time, Pallas kernels for 0%

commit v1 on v0

--- a/solution.py
+++ b/solution.py
@@ -63,8 +63,21 @@
     grad_row = grad_row.reshape(1, proj_size * proj_size).astype(jnp.bfloat16)
     valid_full = lax.all_gather(valid_rows, "dp", axis=1, tiled=True)[0]
     my_index = lax.axis_index("dp")
+
+    def _remake_page(tile_in, link_axis, d_out):
+        vec_out = jnp.concatenate(
+            lax.all_to_all(
+                jnp.stack([tile_in for _ in range(lax.axis_size(link_axis))]),
+                axis_name=link_axis,
+                split_axis=0,
+                concat_axis=0,
+            ),
+            axis=d_out,
+        )
+        return vec_out
+
     scores = lax.dot_general(
-        lax.all_gather(grad_row, "dp", axis=0, tiled=True),
+        _remake_page(grad_row, link_axis="dp", d_out=0),
         valid_full,
         (((1,), (1,)), ((), ())),
         preferred_element_type=jnp.float32,

time: 523 us -> 553 us (1.057)
  the two profiles are of different devices: /device:TPU:4 before, /device:TPU:2 now
where the time goes in v1:
time: 553 us
  waiting for transfers between devices  463 us (84%)
  other arithmetic  46.4 us (8%)
  between operations  13.9 us (3%)
  matrix products  12.7 us (2%)
  starting transfers between devices  10.3 us (2%)
  local copies, waits for them, and re-layouts  6.3 us (1%)
    all_gather x1, waiting for transfers between devices, body(): lax.all_gather(proj_in, 'dp', axis=1, tiled=True)  137 us
    all_gather x1, waiting for transfers between devices, body(): valid_full = lax.all_gather(valid_rows, 'dp', axis=1, tiled=True)[0]  122 us
    all_gather x1, waiting for transfers between devices, body(): lax.all_gather(proj_out, 'dp', axis=1, tiled=True)  93.5 us
    all_gather x1, waiting for transfers between devices, entering(): everything = lax.all_gather(value.astype(jnp.bfloat16), axis)  88.3 us
    select_n x8, other arithmetic, lap(): return jnp.where(reached, new, before)  41.8 us
    all_to_all x1, waiting for transfers between devices, _remake_page(): lax.all_to_all(jnp.stack([tile_in for _ in range(lax.axis_size(link_axis)...  21.1 us
  transfers between devices with their start and end apart: 5, of which 5 were waited for; matrix products, arithmetic and copies ran while one was open for 8% of the time, Pallas kernels for 0%

profile of v1, /device:TPU:2, one launch (start us, length us, event | category | flops | bytes accessed | tf_op | source)
XLA Modules:
  0.0 552.9 jit_solution(13797642606581695799)
XLA Ops:
  6.5 0.7 all-gather.9.cloned.1.call-update
  7.3 0.7 all-gather.5.cloned.1.call-update
  8.0 0.0 all-gather.7.cloned.1.call-start
  8.1 0.7 all-gather.7.cloned.1.call-update
  9.4 136.7 %all-gather.9.cloned.1.call-done = bf16[64,8192]{1,0:T(8,128)(2,1)} async-done(((bf16[64,128]{1,0:T(8,128)(2,1)}), bf16[64,8192]{1,0:T(8,128)(2,1)}) %all-gather.9.cloned.1.call-update) | async-done | bytes 1048592 | tf_op jit(solution)/shard_map/all_gather | solution.py:37
  146.1 2.1 fusion.2
  148.2 88.3 %all-gather.5.cloned.1.call-done = bf16[8,128,8192]{2,1,0:T(8,128)(2,1)} async-done(((bf16[1,128,8192]{2,1,0:T(8,128)(2,1)}), bf16[8,128,8192]{2,1,0:T(8,128)(2,1)}) %all-gather.5.cloned.1.call-update) | async-done | bytes 16777232 | tf_op jit(solution)/shard_map/all_gather | solution.py:11
  236.5 41.8 %while.16 = (s32[]{:T(128)}, f32[128,8192]{1,0:T(8,128)}, s32[]{:T(128)}, bf16[8,128,8192]{2,1,0:T(8,128)(2,1)}, s32[]{:T(128)}, /*index=5*/s32[]{:T(128)}, s32[]{:T(128)}, s32[]{:T(128)}) while((s32[]{:T(128)}, f32[128,8192]{1,0:T(8,128)}, s32[]{:T(128)}, bf16[8,128,8192]{2,1,0:T(8,128)(2,1)}, s32[]{:T(128)}, ...), condition=%wide.region_1.2_spmd.clone, body=%wide.region_0.1_spmd.clone.sunk | while | flops 4194312 | bytes 10485915 | solution.py:20
  236.5 4.1 add_select_fusion.2
  240.6 5.4 add_select_fusion.2
  246.0 5.4 add_select_fusion.2
  251.3 5.4 add_select_fusion.2
  256.7 5.4 add_select_fusion.2
  262.1 5.4 add_select_fusion.2
  267.5 5.4 add_select_fusion.2
  272.9 5.4 add_select_fusion.2
  278.3 93.5 %all-gather.7.cloned.1.call-done = bf16[64,8192]{1,0:T(8,128)(2,1)} async-done(((bf16[64,128]{1,0:T(8,128)(2,1)}), bf16[64,8192]{1,0:T(8,128)(2,1)}) %all-gather.7.cloned.1.call-update) | async-done | bytes 1048592 | tf_op jit(solution)/shard_map/all_gather | solution.py:38
  371.8 5.8 %fusion.4 = f32[128,64]{0,1:T(8,128)S(1)} fusion(bf16[64,8192]{1,0:T(8,128)(2,1)} %all-gather.7.cloned.1.call-done, f32[128,8192]{1,0:T(8,128)} %get-tuple-element.115, bf16[1,128,8192]{2,1,0:T(8,128)(2,1)} %param.10, f32[128]{0:T(128)S(1)} %fusion.12), kind=kOutput, calls=%fused_computation.7 | convolution fusion | flops 807411712 | bytes 7373312 | tf_op jit(solution)/shard_map/dot_general | solution.py:44
  377.6 0.2 convolution_convert_fusion
  377.8 0.1 convert_element_type.44
  377.9 1.0 stack.2
  378.9 0.5 broadcast.25
  379.4 4.6 reduce
  384.0 2.2 reshape.32
  386.2 10.2 %all-to-all-start = ((bf16[64,2,2048]{2,1,0:T(2,128)(2,1)}), bf16[64,2,2048]{2,1,0:T(2,128)(2,1)S(1)}, u32[]{:S(2)}, u32[]{:S(2)}) async-start(bf16[64,2,2048]{2,1,0:T(2,128)(2,1)} %reshape.32), calls=%async_computation | async-start | bytes 1048576 | tf_op jit(solution)/shard_map/all_to_all | solution.py:69
  396.5 0.0 all-gather.11.cloned.1.call-start
  396.5 0.6 copy.9
  397.2 21.1 %all-to-all-done = bf16[64,2,2048]{2,1,0:T(2,128)(2,1)S(1)} async-done(((bf16[64,2,2048]{2,1,0:T(2,128)(2,1)}), bf16[64,2,2048]{2,1,0:T(2,128)(2,1)S(1)}, u32[]{:S(2)}, u32[]{:S(2)}) %all-to-all-start) | async-done | bytes 524320 | tf_op jit(solution)/shard_map/all_to_all | solution.py:69
  418.3 1.8 reshape.33
  420.1 121.6 %all-gather.11.cloned.1.call-done = bf16[1,128,4096]{2,0,1:T(2,128)(2,1)} async-done(((bf16[1,2,4096]{2,0,1:T(2,128)(2,1)}), bf16[1,128,4096]{2,0,1:T(2,128)(2,1)}) %all-gather.11.cloned.1.call-update) | async-done | bytes 1048592 | tf_op jit(solution)/shard_map/all_gather | solution.py:64
  541.8 3.6 fusion.5
  545.4 1.0 convolution_bitcast_fusion
  (12 shorter events, 0.1 us)
Async XLA Ops:
  6.5 139.6 %copy-start = (bf16[1,128,8192]{2,1,0:T(8,128)(2,1)S(1)}, bf16[1,128,8192]{2,1,0:T(8,128)(2,1)}, u32[]{:S(2)}) copy-start(bf16[1,128,8192]{2,1,0:T(8,128)(2,1)} %param.9) | copy-start | bytes 6291460
  6.5 139.6 %all-gather.9.cloned.1.call-start = ((), (), s32[]{:S(2)}) async-start(), calls=%async_computation.3 | async-start | bytes 1064960 | tf_op jit(solution)/shard_map/all_gather | solution.py:37
  7.3 229.2 %all-gather.5.cloned.1.call-start = ((), (), s32[]{:S(2)}) async-start(), calls=%async_computation.1 | async-start | bytes 18874368 | tf_op jit(solution)/shard_map/all_gather | solution.py:11
  8.0 363.8 %all-gather.7.cloned.1.call-start = ((), (), s32[]{:S(2)}) async-start(), calls=%async_computation.2 | async-start | bytes 1064960 | tf_op jit(solution)/shard_map/all_gather | solution.py:38
  377.6 18.9 %copy-start.1 = (bf16[1,2,4096]{2,1,0:T(2,128)(2,1)S(1)}, bf16[1,2,4096]{2,1,0:T(2,128)(2,1)}, u32[]{:S(2)}) copy-start(bf16[1,2,4096]{2,1,0:T(2,128)(2,1)} %param.13) | copy-start | bytes 49156
  377.6 19.6 %copy-start.2 = (s32[64]{0:T(128)S(1)}, s32[64]{0:T(128)}, u32[]{:S(2)}) copy-start(s32[64]{0:T(128)} %param.15) | copy-start | bytes 772
  386.2 32.1 %all-to-all-start = ((bf16[64,2,2048]{2,1,0:T(2,128)(2,1)}), bf16[64,2,2048]{2,1,0:T(2,128)(2,1)S(1)}, u32[]{:S(2)}, u32[]{:S(2)}) async-start(bf16[64,2,2048]{2,1,0:T(2,128)(2,1)} %reshape.32), calls=%async_computation | async-start | bytes 1048576 | tf_op jit(solution)/shard_map/all_to_all | solution.py:69
  396.5 145.3 %all-gather.11.cloned.1.call-start = ((), (), s32[]{:S(2)}) async-start(), calls=%async_computation.4 | async-start | bytes 2129920 | tf_op jit(solution)/shard_map/all_gather | solution.py:64
Sparse Core Ops, SparseCore 0:
  10.3 135.7 all-gather.8
  148.2 88.1 all-gather.4
  239.4 132.3 all-gather.6
  399.9 141.7 all-gather.10
